TPU v7x, 1024 devices: a whole 4x4x32 slice. The times are simulated.
1024 devices in a mesh: row: 32 (over x, y, core), col: 32 (over z).
Axes of the slice: x: 4, y: 4, z: 32, core: 2. Of those that a mesh axis runs over, the one named last changes fastest.
Arguments:
- tokens: bfloat16 [512, 12288], P('row', 'col'), may hold values from -6 to 6
- w_in: bfloat16 [12288, 24576], P('col', 'row'), may hold values from -0.0546875 to 0.0546875
- w_out: bfloat16 [24576, 12288], P('row', 'col'), may hold values from -0.0390625 to 0.0390625
- cotangent: bfloat16 [512, 12288], P('row', 'col'), may hold values from -6 to 6
Outputs:
- output: bfloat16 [512, 12288], P('row', 'col')
- grad_tokens: bfloat16 [512, 12288], P('row', 'col')
- grad_in: float32 [12288, 24576], P('col', 'row')
- grad_out: float32 [24576, 12288], P('row', 'col')
All inputs are finite; a program needn't handle non-finite values.
Results may differ from a plain program's by a relative error of at most 0.0033.
Values may be sent and summed in bfloat16 or wider, within the bound.
A program may use at most 32 MiB of HBM per device.

v0:
```python
import jax
import jax.numpy as jnp
from jax import lax
from jax.sharding import PartitionSpec as P

slope_c = 0.7978845608028654
cubic_k = 0.044715


def gelu_value(h):
    inner = slope_c * (h + cubic_k * h * h * h)
    return 0.5 * h * (1.0 + jnp.tanh(inner))


def gelu_slope(h):
    inner = slope_c * (h + cubic_k * h * h * h)
    tval = jnp.tanh(inner)
    return 0.5 * (1.0 + tval) + 0.5 * h * (1.0 - tval * tval) * slope_c * (
        1.0 + 3.0 * cubic_k * h * h
    )


def product(left, right, contract):
    return lax.dot_general(
        left, right, (((1,), (contract,)), ((), ())), preferred_element_type=jnp.float32
    )


def contract_first(left, right):
    return lax.dot_general(
        left, right, (((0,), (0,)), ((), ())), preferred_element_type=jnp.float32
    )


def column_reduce(left, right, contract):
    return lax.psum_scatter(product(left, right, contract), "col", scatter_dimension=0, tiled=True)


def row_reduce(left, right, contract):
    return lax.psum_scatter(product(left, right, contract), "row", scatter_dimension=0, tiled=True)


def hidden_gather(values):
    return lax.all_gather(values, "col", axis=0, tiled=True)


def on_device(tokens, w_in, w_out, cotangent):
    tok_all, cot_all = (
        lax.all_gather(tokens, "row", axis=0, tiled=True),
        lax.all_gather(cotangent, "row", axis=0, tiled=True),
    )
    dact_share = None
    pre_share = column_reduce(tok_all, w_in, 0)
    act_all = hidden_gather(gelu_value(pre_share).astype(jnp.bfloat16))
    mixed = row_reduce(act_all, w_out, 0)
    output = (tokens.astype(jnp.float32) + mixed).astype(jnp.bfloat16)
    dact_share = column_reduce(cot_all, w_out, 1)
    dpre_share = (dact_share * gelu_slope(pre_share)).astype(jnp.bfloat16)
    dpre_all = hidden_gather(dpre_share)
    grad_out = contract_first(act_all, cot_all)
    grad_in = contract_first(tok_all, dpre_all)
    back = row_reduce(dpre_all, w_in, 1)
    grad_tokens = (cotangent.astype(jnp.float32) + back).astype(jnp.bfloat16)
    return (output, grad_tokens, grad_in, grad_out)


def solution(mesh):
    return jax.shard_map(
        on_device,
        mesh=mesh,
        in_specs=(P("row", "col"), P("col", "row"), P("row", "col"), P("row", "col")),
        out_specs=(P("row", "col"), P("row", "col"), P("col", "row"), P("row", "col")),
        check_vma=False,
    )
```

profile of v0, /device:TPU:1, one launch (start us, length us, event | category | flops | bytes accessed | tf_op | source)
XLA Modules:
  0.0 643.0 jit_solution(16742464133222934142)
XLA Ops:
  7.2 0.0 copy-start
  7.2 0.0 reduce-scatter.9.cloned.1.call-start
  7.2 36.6 %all_gather.14 = bf16[512,384]{1,0:T(8,128)(2,1)S(1)} all-gather(bf16[16,384]{1,0:T(8,128)(2,1)} %param.7), channel_id=1, replica_groups=mesh['row'=32,'col'=32] {'row'}, dimensions={0}, use_global_device_ids=true | all-gather | bytes 405504 | tf_op jit(solution)/shard_map/all_gather | solution.py:50
  43.9 0.0 copy-start.1
  43.9 0.7 copy-done.1
  44.6 0.0 copy-done
  44.6 1.7 fusion.9
  46.3 0.0 copy-start.5
  46.3 0.0 copy-start.4
  46.4 0.0 reduce-scatter.9.cloned.1.call-update
  46.4 0.0 reduce-scatter.5.cloned.1.call-start
  46.4 0.6 copy-done.5
  47.1 24.3 %all_gather.12 = bf16[512,384]{1,0:T(8,128)(2,1)S(1)} all-gather(bf16[16,384]{1,0:T(8,128)(2,1)S(1)} %copy-done.5), channel_id=1, replica_groups=mesh['row'=32,'col'=32] {'row'}, dimensions={0}, use_global_device_ids=true | all-gather | bytes 405504 | tf_op jit(solution)/shard_map/all_gather | solution.py:49
  71.3 0.0 copy-start.3
  71.3 0.7 copy-done.3
  72.1 0.0 copy-done.4
  72.1 1.7 fusion.7
  73.8 0.0 reduce-scatter.5.cloned.1.call-update
  73.8 0.0 reduce-scatter.7.cloned.1.call-start
  73.9 81.3 %reduce-scatter.9.cloned.1.call-done = f32[16,768]{1,0:T(8,128)} async-done(((f32[512,768]{1,0:T(8,128)}), f32[16,768]{1,0:T(8,128)}) %reduce-scatter.9.cloned.1.call-update) | async-done | bytes 49168 | tf_op jit(solution)/shard_map/reduce_scatter | solution.py:36
  155.2 135.1 %reduce-scatter.5.cloned.1.call-done = f32[16,768]{1,0:T(8,128)} async-done(((f32[512,768]{1,0:T(8,128)}), f32[16,768]{1,0:T(8,128)}) %reduce-scatter.5.cloned.1.call-update) | async-done | bytes 49168 | tf_op jit(solution)/shard_map/reduce_scatter | solution.py:36
  290.2 0.9 fusion.6
  291.1 44.8 %all_gather.13 = bf16[512,768]{1,0:T(8,128)(2,1)S(1)} all-gather(bf16[16,768]{1,0:T(8,128)(2,1)S(1)} %get-tuple-element.9), channel_id=1, replica_groups=mesh['row'=32,'col'=32] {'col'}, dimensions={0}, use_global_device_ids=true | all-gather | bytes 811008 | tf_op jit(solution)/shard_map/all_gather | solution.py:44
  335.9 1.5 fusion.8
  337.4 0.0 reduce-scatter.7.cloned.1.call-update
  337.4 0.0 reduce-scatter.11.cloned.1.call-start
  337.4 43.3 %all_gather.15 = bf16[512,768]{1,0:T(8,128)(2,1)S(1)} all-gather(bf16[16,768]{1,0:T(8,128)(2,1)S(1)} %get-tuple-element.8), channel_id=1, replica_groups=mesh['row'=32,'col'=32] {'col'}, dimensions={0}, use_global_device_ids=true | all-gather | bytes 811008 | tf_op jit(solution)/shard_map/all_gather | solution.py:44
  380.7 1.5 fusion.10
  382.2 0.0 reduce-scatter.11.cloned.1.call-update
  382.2 1.6 convolution_bitcast_fusion
  383.8 0.0 copy-start.2
  383.8 1.4 copy.8
  385.2 0.0 copy-done.2
  385.2 0.0 copy-start.6
  385.2 1.6 fusion.11
  386.8 111.9 %reduce-scatter.7.cloned.1.call-done = f32[16,384]{1,0:T(8,128)} async-done(((f32[512,384]{1,0:T(8,128)}), f32[16,384]{1,0:T(8,128)}) %reduce-scatter.7.cloned.1.call-update) | async-done | bytes 24592 | tf_op jit(solution)/shard_map/reduce_scatter | solution.py:40
  498.7 1.3 add_convert_fusion.1
  500.0 135.1 %reduce-scatter.11.cloned.1.call-done = f32[16,384]{1,0:T(8,128)} async-done(((f32[512,384]{1,0:T(8,128)}), f32[16,384]{1,0:T(8,128)}) %reduce-scatter.11.cloned.1.call-update) | async-done | bytes 24592 | tf_op jit(solution)/shard_map/reduce_scatter | solution.py:40
  635.1 0.0 copy-done.6
  635.1 1.3 add_convert_fusion
Async XLA Ops:
  7.2 37.4 %copy-start = (bf16[768,384]{1,0:T(8,128)(2,1)S(1)}, bf16[768,384]{1,0:T(8,128)(2,1)}, u32[]{:S(2)}) copy-start(bf16[768,384]{1,0:T(8,128)(2,1)} %param.6) | copy-start | bytes 1769476
  7.2 148.0 %reduce-scatter.9.cloned.1.call-start = ((), (), s32[]{:S(2)}) async-start(), calls=%async_computation.6 | async-start | bytes 1622016 | tf_op jit(solution)/shard_map/reduce_scatter | solution.py:36
  43.9 0.7 copy-start.1
  46.3 0.7 copy-start.5
  46.3 25.7 %copy-start.4 = (bf16[384,768]{1,0:T(8,128)(2,1)S(1)}, bf16[384,768]{1,0:T(8,128)(2,1)}, u32[]{:S(2)}) copy-start(bf16[384,768]{1,0:T(8,128)(2,1)} %param.5) | copy-start | bytes 1769476
  46.4 243.9 %reduce-scatter.5.cloned.1.call-start = ((), (), s32[]{:S(2)}) async-start(), calls=%async_computation.4 | async-start | bytes 1622016 | tf_op jit(solution)/shard_map/reduce_scatter | solution.py:36
  71.3 0.7 copy-start.3
  73.8 424.9 %reduce-scatter.7.cloned.1.call-start = ((), (), s32[]{:S(2)}) async-start(), calls=%async_computation.5 | async-start | bytes 811008 | tf_op jit(solution)/shard_map/reduce_scatter | solution.py:40
  337.4 297.7 %reduce-scatter.11.cloned.1.call-start = ((), (), s32[]{:S(2)}) async-start(), calls=%async_computation.7 | async-start | bytes 811008 | tf_op jit(solution)/shard_map/reduce_scatter | solution.py:40
  383.8 1.4 copy-start.2
  385.2 249.9 %copy-start.6 = (bf16[16,384]{1,0:T(8,128)(2,1)S(1)}, bf16[16,384]{1,0:T(8,128)(2,1)}, u32[]{:S(2)}) copy-start(bf16[16,384]{1,0:T(8,128)(2,1)} %param.7) | copy-start | bytes 36868
Sparse Core Ops, SparseCore 0:
  46.5 108.6 reduce-scatter.8
  158.9 131.2 reduce-scatter.4
  337.5 161.1 reduce-scatter.6
  504.0 130.9 reduce-scatter.10
where the time goes:
time: 644 us; the launch traced here: 643 us
  waiting for transfers between devices  463 us (72%)
  blocking collectives  149 us (23%)
  between operations  13.8 us (2%)
  matrix products  9.62 us (1%)
    reduce_scatter x2, waiting for transfers between devices, row_reduce(): lax.psum_scatter(product(left, right, contract), 'row', scatter_dimension...  247 us
    reduce_scatter x2, waiting for transfers between devices, column_reduce(): lax.psum_scatter(product(left, right, contract), 'col', scatter_dimension...  216 us
    all_gather x2, blocking collectives, hidden_gather(): return lax.all_gather(values, 'col', axis=0, tiled=True)  88.1 us
    all_gather x1, blocking collectives, on_device(): lax.all_gather(cotangent, 'row', axis=0, tiled=True)  36.6 us
    all_gather x1, blocking collectives, on_device(): lax.all_gather(tokens, 'row', axis=0, tiled=True)  24.3 us
  transfers between devices with their start and end apart: 4, of which 4 were waited for; matrix products, arithmetic and copies ran while one was open for 1% of the time, Pallas kernels for 0%

commit v1 on v0

v1 whole, which is shorter than its diff:
```python
import functools

import jax
import jax.numpy as jnp
from jax import lax
from jax.experimental import pallas as pl
from jax.experimental.pallas import tpu as pltpu
from jax.sharding import PartitionSpec as P

slope_c = 0.7978845608028654
cubic_k = 0.044715
MESH = pl.DeviceIdType.MESH
SCALE = 2.0**20
BF = jnp.bfloat16
F32 = jnp.float32


def gelu_both(h):
    tval = jnp.tanh(slope_c * (h + cubic_k * h * h * h))
    value = 0.5 * h * (1.0 + tval)
    slope = 0.5 * (1.0 + tval) + 0.5 * h * (1.0 - tval * tval) * slope_c * (
        1.0 + 3.0 * cubic_k * h * h
    )
    return value, slope


def encode(x):
    a = x * SCALE
    a = a * a
    a = a * a
    return jnp.where(x < 0.0, -a, a).astype(BF)


def decode(y):
    y = y.astype(F32)
    a = jnp.sqrt(jnp.sqrt(jnp.abs(y))) * (1.0 / SCALE)
    return jnp.where(y < 0.0, -a, a)


def mm(left, right, dims):
    return lax.dot_general(left, right, (dims, ((), ())), preferred_element_type=F32)


NN = ((1,), (0,))
NT = ((1,), (1,))
TN = ((0,), (0,))


def kernel(
    nz, dims, T,
    tok_ref, cot_ref, win_ref, wout_ref,
    out_ref, gtok_ref, gin_ref, gout_ref,
    own, tc, win, wout, part, zsend, zrecv, hid, osend, orecv,
    load_sem, gsend_sem, grecv_sem, zsend_sem, zrecv_sem, hsend_sem, hrecv_sem, osend_sem, orecv_sem,
):
    row, z = lax.axis_index("row"), lax.axis_index("col")
    X, Y, C = dims
    S = nz // 2

    def digits(i):
        return lax.div(i, Y * C), lax.rem(lax.div(i, C), Y), lax.rem(i, C)

    rx, ry, rc = digits(row)

    def plus(o):
        ox, oy, oc = digits(o)
        return (lax.rem(rx + ox, X) * Y + lax.rem(ry + oy, Y)) * C + lax.rem(rc + oc, C)

    def minus(o):
        ox, oy, oc = digits(o)
        return (lax.rem(rx - ox + X, X) * Y + lax.rem(ry - oy + Y, Y)) * C + lax.rem(rc - oc + C, C)

    def owner(p):
        half = lax.div(p + 1, 2)
        off = jnp.where(lax.rem(p, 2) == 0, S - half, half - S)
        return lax.rem(z + off + nz, nz)

    def rows(p, n=1):
        return pl.ds(pl.multiple_of(p * T, T), n * T)

    right, left = lax.rem(z + 1, nz), lax.rem(z + nz - 1, nz)
    side = (right, left)

    for i, (src, dst) in enumerate(
        ((tok_ref, own.at[0]), (cot_ref, own.at[1]), (win_ref, win), (wout_ref, wout))
    ):
        pltpu.make_async_copy(src, dst, load_sem.at[i]).start()

    barrier = pltpu.get_barrier_semaphore()
    for d in range(2):
        pl.semaphore_signal(barrier, inc=1, device_id=(row, side[d]), device_id_type=MESH)

    @pl.loop(1, nz)
    def _(o):
        pl.semaphore_signal(barrier, inc=1, device_id=(plus(o), z), device_id_type=MESH)

    for i, (src, dst) in enumerate(((tok_ref, own.at[0]), (cot_ref, own.at[1]))):
        pltpu.make_async_copy(src, dst, load_sem.at[i]).wait()
    pl.semaphore_wait(barrier, nz + 1)

    def gather(p, peer):
        return pltpu.make_async_remote_copy(
            src_ref=own, dst_ref=tc.at[:, rows(p)],
            send_sem=gsend_sem.at[p], recv_sem=grecv_sem.at[p],
            device_id=(peer, z), device_id_type=MESH,
        )

    def gather_self(p):
        return pltpu.make_async_copy(own, tc.at[:, rows(p)], grecv_sem.at[p])

    @pl.loop(0, nz)
    def _(p):
        o = owner(p)

        @pl.when(o != 0)
        def _():
            gather(p, minus(o)).start()

        @pl.when(o == 0)
        def _():
            gather_self(p).start()

    for i, (src, dst) in ((2, (win_ref, win)), (3, (wout_ref, wout))):
        pltpu.make_async_copy(src, dst, load_sem.at[i]).wait()

    def partials(lo, hi):
        @pl.loop(lo, hi)
        def _(p):
            gather_self(p).wait()

        r = slice(lo * T, hi * T)
        part[0, r, :] = mm(tc[0, r, :], win[...], NN)
        part[1, r, :] = mm(tc[1, r, :], wout[...], NT)

    def zcopy(d, i, s):
        return pltpu.make_async_remote_copy(
            src_ref=zsend.at[d, i, rows(s - 1)], dst_ref=zrecv.at[d, i, rows(s - 1)],
            send_sem=zsend_sem.at[d, i, s - 1], recv_sem=zrecv_sem.at[d, i, s - 1],
            device_id=(row, side[d]), device_id_type=MESH,
        )

    def zstep(s, both, first=False):
        for i in range(2):
            for d in range(both):
                value = part[i, rows(2 * (s - 1) + d), :]
                if not first:
                    zcopy(d, i, s - 1).wait_recv()
                    value = value + decode(zrecv[d, i, rows(s - 2), :])
                zsend[d, i, rows(s - 1), :] = encode(value)
                zcopy(d, i, s).start()

    bounds = sorted({b for b in (1, 2, 5, 9, 13) if b <= S} | {S + 1})
    groups = [(a, b) for a, b in zip(bounds[:-1], bounds[1:])]
    place = {}
    for a, b in groups[1:]:
        place.setdefault(max(1, a - 2), []).append((2 * (a - 1), 2 * (b - 1)))
    partials(0, 2 * (groups[0][1] - 1))
    zstep(1, 2 if S > 1 else 1, True)
    done = 1
    for at in sorted(place):
        if at > done:
            pl.loop(done + 1, at + 1)(lambda s: zstep(s, 2))
            done = at
        for g in place[at]:
            partials(*g)
    if S - 1 > done:
        pl.loop(done + 1, S)(lambda s: zstep(s, 2))
    if S > 1:
        zstep(S, 1)

    def hslot(d, s):
        return nz - 2 * s - (1 - d)

    def hmove(d, i, s):
        src = nz - 1 if isinstance(s, int) and s == 1 else hslot(d, s - 1)
        return pltpu.make_async_remote_copy(
            src_ref=hid.at[i, rows(src)], dst_ref=hid.at[i, rows(hslot(d, s))],
            send_sem=hsend_sem.at[d, i, s - 1], recv_sem=hrecv_sem.at[d, i, s - 1],
            device_id=(row, side[d]), device_id_type=MESH,
        )

    own_rows = rows(nz - 1)
    slope = None
    for i in range(2):
        value = part[i, own_rows, :]
        for d, s in ((0, S), (1, S - 1)):
            if s >= 1:
                zcopy(d, i, s).wait_recv()
                value = value + decode(zrecv[d, i, rows(s - 1), :])
        if i == 0:
            value, slope = gelu_both(value)
        else:
            value = value * slope
        hid[i, own_rows, :] = value.astype(BF)
        for d in ((1, 0) if S > 1 else (1,)):
            hmove(d, i, 1).start()

    def ocopy(p, peer):
        return pltpu.make_async_remote_copy(
            src_ref=osend.at[:, rows(p)], dst_ref=orecv.at[:, rows(p)],
            send_sem=osend_sem.at[p], recv_sem=orecv_sem.at[p],
            device_id=(peer, z), device_id_type=MESH,
        )

    def ocopy_self(p):
        return pltpu.make_async_copy(osend.at[:, rows(p)], orecv.at[:, rows(p)], orecv_sem.at[p])

    def products(lo, hi):
        r = slice(lo * T, hi * T)
        osend[0, r, :] = mm(hid[0, r, :], wout[...], NN).astype(BF)
        osend[1, r, :] = mm(hid[1, r, :], win[...], NT).astype(BF)

        @pl.loop(lo, hi)
        def _(j):
            p = lo + hi - 1 - j
            o = owner(p)

            @pl.when(o != 0)
            def _():
                ocopy(p, plus(o)).start()

            @pl.when(o == 0)
            def _():
                ocopy_self(p).start()

    W = 128
    pieces = [(0, k) for k in range(gout_ref.shape[0] // W)] + [(1, k) for k in range(gin_ref.shape[0] // W)]
    half = nz // 2 * T

    def grad_piece(piece, r, add):
        which, k = piece
        c = slice(k * W, (k + 1) * W)
        if which == 0:
            ref, value = gout_ref, mm(hid[0, r, c], tc[1, r, :], TN)
        else:
            ref, value = gin_ref, mm(tc[0, r, c], hid[1, r, :], TN)
        ref[c, :] = ref[c, :] + value if add else value

    ends = sorted({e for e in (3, 7, 11, 14, 15) if e < S} | {S})
    top = nz
    waiting = list(pieces)
    for s in range(1, S + 1):
        for i in range(2):
            for d in ((1, 0) if s < S else (1,)):
                hmove(d, i, s).wait_recv()
                if s + (1 - d) < S:
                    hmove(d, i, s + 1).start()
        if s in ends:
            low = nz - 1 - 2 * s if s < S else 0
            products(low, top)
            top = low
        if 2 * s >= S + 1 and s < S and waiting:
            grad_piece(waiting.pop(0), slice(half, 2 * half), False)
    for piece in waiting:
        grad_piece(piece, slice(half, 2 * half), False)
    for piece in pieces:
        grad_piece(piece, slice(0, half), True)

    for p in range(nz):
        ocopy_self(p).wait()
    for i, (mine, ref) in enumerate(((own, out_ref), (own, gtok_ref))):
        total = own[i].astype(F32)
        for p in range(nz):
            total = total + orecv[i, rows(p), :].astype(F32)
        ref[...] = total.astype(BF)

    @pl.loop(0, nz)
    def _(p):
        @pl.when(owner(p) != 0)
        def _():
            gather(p, row).wait_send()
            ocopy(p, row).wait_send()

    for i in range(2):
        for d in range(2):
            @pl.loop(1, S + 1 - d)
            def _(s):
                zcopy(d, i, s).wait_send()

            @pl.loop(1, S + d)
            def _(s):
                pltpu.make_async_remote_copy(
                    src_ref=hid.at[i, rows(0)], dst_ref=hid.at[i, rows(0)],
                    send_sem=hsend_sem.at[d, i, s - 1], recv_sem=hrecv_sem.at[d, i, s - 1],
                    device_id=(row, side[d]), device_id_type=MESH,
                ).wait_send()


def on_device(nz, dims, tokens, w_in, w_out, cotangent):
    T, DL = tokens.shape
    HL = w_in.shape[1]
    S = nz // 2
    any_space = pl.BlockSpec(memory_space=pl.ANY)
    vmem = pl.BlockSpec(memory_space=pltpu.VMEM)
    dma = pltpu.SemaphoreType.DMA
    flops = 2 * 6 * nz * T * DL * HL
    return pl.pallas_call(
        functools.partial(kernel, nz, dims, T),
        out_shape=(
            jax.ShapeDtypeStruct((T, DL), BF),
            jax.ShapeDtypeStruct((T, DL), BF),
            jax.ShapeDtypeStruct((DL, HL), F32),
            jax.ShapeDtypeStruct((HL, DL), F32),
        ),
        in_specs=[any_space] * 4,
        out_specs=(vmem,) * 4,
        scratch_shapes=[
            pltpu.VMEM((2, T, DL), BF),
            pltpu.VMEM((2, nz * T, DL), BF),
            pltpu.VMEM((DL, HL), BF),
            pltpu.VMEM((HL, DL), BF),
            pltpu.VMEM((2, nz * T, HL), F32),
            pltpu.VMEM((2, 2, S * T, HL), BF),
            pltpu.VMEM((2, 2, S * T, HL), BF),
            pltpu.VMEM((2, nz * T, HL), BF),
            pltpu.VMEM((2, nz * T, DL), BF),
            pltpu.VMEM((2, nz * T, DL), BF),
            dma((4,)),
            dma((nz,)),
            dma((nz,)),
            dma((2, 2, S)),
            dma((2, 2, S)),
            dma((2, 2, S)),
            dma((2, 2, S)),
            dma((nz,)),
            dma((nz,)),
        ],
        compiler_params=pltpu.CompilerParams(
            collective_id=0, has_side_effects=True, vmem_limit_bytes=40 * 2**20
        ),
        cost_estimate=pl.CostEstimate(flops=flops, bytes_accessed=4 * DL * HL * 3, transcendentals=0),
    )(tokens, cotangent, w_in, w_out)


def solution(mesh):
    nz = mesh.shape["col"]
    dims = {32: (4, 4, 2), 8: (2, 2, 2), 4: (1, 2, 2)}[mesh.shape["row"]]
    return jax.shard_map(
        functools.partial(on_device, nz, dims),
        mesh=mesh,
        in_specs=(P("row", "col"), P("col", "row"), P("row", "col"), P("row", "col")),
        out_specs=(P("row", "col"), P("row", "col"), P("col", "row"), P("row", "col")),
        check_vma=False,
    )
```

time: 644 us -> 148 us (0.23)
  waiting for transfers between devices: 463 us -> 0 us
  blocking collectives: 149 us -> 0 us
  Pallas kernels: 0 us -> 139 us
  between operations: 13.8 us -> 0.65 us
  matrix products: 9.62 us -> 0 us
    reduce_scatter x4 -> x0, waiting for transfers between devices: 463 us -> none  [the longest x2 247 us: row_reduce(): lax.psum_scatter(product(left, right, contract), 'row', scatter_dimension...]
    all_gather x4 -> x0, blocking collectives: 149 us -> none  [the longest x2 88.1 us: hidden_gather(): return lax.all_gather(values, 'col', axis=0, tiled=True)]
    pallas_call x0 -> x1, Pallas kernels: none -> 139 us  [on_device(): pl.pallas_call(functools.partial(kernel, nz, dims, T), out_shape=(jax.Sha...]
    dot_general x6 -> x0, matrix products: 9.62 us -> none  [the longest x4 6.42 us: product(): lax.dot_general(left, right, (((1,), (contract,)), ((), ())), preferred_e...]
  transfers between devices with their start and end apart: 4 -> 0, of which waited for: 4 -> 0; matrix products, arithmetic and copies ran while one was open for 1% -> 0% of each run, Pallas kernels for 0% -> 0%
where the time goes in v1:
time: 148 us; the launch traced here: 146 us
  Pallas kernels  139 us (94%)
  local copies, waits for them, and re-layouts  6.76 us (5%)
    pallas_call x1, Pallas kernels, on_device(): pl.pallas_call(functools.partial(kernel, nz, dims, T), out_shape=(jax.Sha...  139 us
    unnamed x12, local copies, waits for them, and re-layouts  6.76 us

profile of v1, /device:TPU:1, one launch (start us, length us, event | category | flops | bytes accessed | tf_op | source)
XLA Modules:
  0.0 146.0 jit_solution(3045238759743803945)
XLA Ops:
  0.6 0.0 copy-start
  0.6 1.1 copy-done
  1.7 0.0 copy-start.1
  1.7 1.1 copy-done.1
  2.8 0.0 copy-start.2
  2.8 0.7 copy-done.2
  3.5 0.0 copy-start.3
  3.5 0.7 copy-done.3
  4.2 138.6 %shard_map.75 = (bf16[16,384]{1,0:T(8,128)(2,1)S(1)}, bf16[16,384]{1,0:T(8,128)(2,1)S(1)}, f32[384,768]{1,0:T(8,128)S(1)}, f32[768,384]{1,0:T(8,128)S(1)}) custom-call(bf16[16,384]{1,0:T(8,128)(2,1)S(1)} %copy-done.2, bf16[16,384]{1,0:T(8,128)(2,1)S(1)} %copy-done.3, bf16[384,768]{1,0:T(8,128)(2,1)S(1)} %copy-done, bf16[768,384]{1,0:T(8,128)(2,1)S(1)} %copy-done.1), custom_call_target="tpu_custom_call" | custom-call | flops 1811939328 | bytes 3538944 | tf_op jit(solution)/shard_map/pallas_call | solution.py:297
  142.7 0.6 copy.12
  143.3 0.6 copy.13
  143.9 1.0 copy.14
  145.0 1.0 copy.15
Async XLA Ops:
  0.6 1.1 copy-start
  1.7 1.1 copy-start.1
  2.8 0.7 copy-start.2
  3.5 0.7 copy-start.3

commit v2 on v1

v2 whole, which is shorter than its diff:
```python
import functools

import jax
import jax.numpy as jnp
from jax import lax
from jax.experimental import pallas as pl
from jax.experimental.pallas import tpu as pltpu
from jax.sharding import PartitionSpec as P

slope_c = 0.7978845608028654
cubic_k = 0.044715
MESH = pl.DeviceIdType.MESH
SCALE = 2.0**20
BF = jnp.bfloat16
F32 = jnp.float32


def gelu_both(h):
    tval = jnp.tanh(slope_c * (h + cubic_k * h * h * h))
    value = 0.5 * h * (1.0 + tval)
    slope = 0.5 * (1.0 + tval) + 0.5 * h * (1.0 - tval * tval) * slope_c * (
        1.0 + 3.0 * cubic_k * h * h
    )
    return value, slope


def encode(x):
    a = x * SCALE
    a = a * a
    a = a * a
    return jnp.where(x < 0.0, -a, a).astype(BF)


def decode(y):
    y = y.astype(F32)
    a = jnp.sqrt(jnp.sqrt(jnp.abs(y))) * (1.0 / SCALE)
    return jnp.where(y < 0.0, -a, a)


def mm(left, right, dims):
    return lax.dot_general(left, right, (dims, ((), ())), preferred_element_type=F32)


NN = ((1,), (0,))
NT = ((1,), (1,))
TN = ((0,), (0,))


def kernel(
    nz, dims, T,
    tok_ref, cot_ref, win_ref, wout_ref,
    out_ref, gtok_ref, gin_ref, gout_ref,
    own, tc, win, wout, part, zsend, zrecv, hid, osend, orecv, gin, gout, ends,
    load_sem, gsend_sem, grecv_sem, zsend_sem, zrecv_sem, hsend_sem, hrecv_sem, osend_sem, orecv_sem, store_sem,
):
    row, z = lax.axis_index("row"), lax.axis_index("col")
    X, Y, C = dims
    S = nz // 2
    J = S // 2

    def digits(i):
        return lax.div(i, Y * C), lax.rem(lax.div(i, C), Y), lax.rem(i, C)

    rx, ry, rc = digits(row)

    def plus(o):
        ox, oy, oc = digits(o)
        return (lax.rem(rx + ox, X) * Y + lax.rem(ry + oy, Y)) * C + lax.rem(rc + oc, C)

    def minus(o):
        ox, oy, oc = digits(o)
        return (lax.rem(rx - ox + X, X) * Y + lax.rem(ry - oy + Y, Y)) * C + lax.rem(rc - oc + C, C)

    def owner(p):
        half = lax.div(p + 1, 2)
        off = jnp.where(lax.rem(p, 2) == 0, S - half, half - S)
        return lax.rem(z + off + nz, nz)

    def rows(p, n=1):
        return pl.ds(pl.multiple_of(p * T, T), n * T)

    side = (lax.rem(z + 1, nz), lax.rem(z + nz - 1, nz))
    far = (lax.rem(z + 2, nz), lax.rem(z + nz - 2, nz))
    ring = side + (far if nz > 4 else far[:1])

    for i, (src, dst) in enumerate(
        ((tok_ref, own.at[0]), (cot_ref, own.at[1]), (win_ref, win), (wout_ref, wout))
    ):
        pltpu.make_async_copy(src, dst, load_sem.at[i]).start()

    barrier = pltpu.get_barrier_semaphore()
    for peer in ring:
        pl.semaphore_signal(barrier, inc=1, device_id=(row, peer), device_id_type=MESH)

    @pl.loop(1, nz)
    def _(o):
        pl.semaphore_signal(barrier, inc=1, device_id=(plus(o), z), device_id_type=MESH)

    for i, (src, dst) in enumerate(((tok_ref, own.at[0]), (cot_ref, own.at[1]))):
        pltpu.make_async_copy(src, dst, load_sem.at[i]).wait()
    pl.semaphore_wait(barrier, nz - 1 + len(ring))

    def gather(p, peer):
        return pltpu.make_async_remote_copy(
            src_ref=own, dst_ref=tc.at[:, rows(p)],
            send_sem=gsend_sem.at[p], recv_sem=grecv_sem.at[p],
            device_id=(peer, z), device_id_type=MESH,
        )

    def gather_self(p):
        return pltpu.make_async_copy(own, tc.at[:, rows(p)], grecv_sem.at[p])

    @pl.loop(0, nz)
    def _(p):
        o = owner(p)

        @pl.when(o != 0)
        def _():
            gather(p, minus(o)).start()

        @pl.when(o == 0)
        def _():
            gather_self(p).start()

    for i, (src, dst) in ((2, (win_ref, win)), (3, (wout_ref, wout))):
        pltpu.make_async_copy(src, dst, load_sem.at[i]).wait()

    def partials(lo, hi):
        @pl.loop(lo, hi)
        def _(p):
            gather_self(p).wait()

        r = slice(lo * T, hi * T)
        part[0, r, :] = mm(tc[0, r, :], win[...], NN)
        part[1, r, :] = mm(tc[1, r, :], wout[...], NT)

    def zcopy(d, i, slot, peer):
        return pltpu.make_async_remote_copy(
            src_ref=zsend.at[d, i, rows(slot)], dst_ref=zrecv.at[d, i, rows(slot)],
            send_sem=zsend_sem.at[d, i, slot], recv_sem=zrecv_sem.at[d, i, slot],
            device_id=(row, peer[d]), device_id_type=MESH,
        )

    def arrived(d, i, slot):
        zcopy(d, i, slot, side).wait_recv()
        return decode(zrecv[d, i, rows(slot), :])

    def zstep(j, first):
        for i in range(2):
            for d in range(2):
                if first == 0 and d == 1:
                    continue
                value = part[i, rows(4 * j - d), :]
                if first > 0:
                    value = value + arrived(d, i, J + j - 1)
                if first > d:
                    value = value + arrived(d, i, j - 1)
                zsend[d, i, rows(j), :] = encode(value)
                zcopy(d, i, j, far).start()
        for i in range(2):
            for d in range(2):
                zsend[d, i, rows(J + j), :] = encode(part[i, rows(4 * j + 2 - d), :])
                zcopy(d, i, J + j, side).start()

    partials(0, 4)
    zstep(0, 0)
    done = 0
    for lo, hi in ((4, 8), (8, 16), (16, nz)):
        if hi <= nz and lo < hi:
            partials(lo, hi)
            if done + 1 < J:
                done += 1
                zstep(done, min(done, 2))
    if done + 1 < J:
        pl.loop(done + 1, J)(lambda j: zstep(j, 2))

    def hslot(d, k):
        return 2 * (S - k) - 1 + (d if k else 0)

    def hfar(d, i, j):
        return pltpu.make_async_remote_copy(
            src_ref=hid.at[i, rows(hslot(d, 2 * j))], dst_ref=hid.at[i, rows(hslot(d, 2 * j + 2))],
            send_sem=hsend_sem.at[d, i, j], recv_sem=hrecv_sem.at[d, i, j],
            device_id=(row, far[d]), device_id_type=MESH,
        )

    def hnear(d, i, j):
        return pltpu.make_async_remote_copy(
            src_ref=hid.at[i, rows(hslot(d, 2 * j))], dst_ref=hid.at[i, rows(hslot(d, 2 * j + 1))],
            send_sem=hsend_sem.at[d, i, J + j], recv_sem=hrecv_sem.at[d, i, J + j],
            device_id=(row, side[d]), device_id_type=MESH,
        )

    def last(d):
        return J - 1 + d

    def forward(i, j):
        for d in (1, 0):
            if j > 0 and j <= last(d):
                hfar(d, i, j - 1).wait_recv()
            if j < last(d):
                hfar(d, i, j).start()
            if j < J:
                hnear(d, i, j).start()

    own_rows = rows(nz - 1)
    slope = None
    for i in range(2):
        value = part[i, own_rows, :]
        for d in range(2):
            value = value + arrived(d, i, 2 * J - 1)
            if J - 1 >= d:
                value = value + arrived(d, i, J - 1)
        if i == 0:
            value, slope = gelu_both(value)
        else:
            value = value * slope
        hid[i, own_rows, :] = value.astype(BF)
        forward(i, 0)

    def ocopy(p, peer):
        return pltpu.make_async_remote_copy(
            src_ref=osend.at[:, rows(p)], dst_ref=orecv.at[:, rows(p)],
            send_sem=osend_sem.at[p], recv_sem=orecv_sem.at[p],
            device_id=(peer, z), device_id_type=MESH,
        )

    def ocopy_self(p):
        return pltpu.make_async_copy(osend.at[:, rows(p)], orecv.at[:, rows(p)], orecv_sem.at[p])

    def products(lo, hi):
        r = slice(lo * T, hi * T)
        osend[0, r, :] = mm(hid[0, r, :], wout[...], NN).astype(BF)
        osend[1, r, :] = mm(hid[1, r, :], win[...], NT).astype(BF)

        @pl.loop(lo, hi)
        def _(j):
            p = lo + hi - 1 - j
            o = owner(p)

            @pl.when(o != 0)
            def _():
                ocopy(p, plus(o)).start()

            @pl.when(o == 0)
            def _():
                ocopy_self(p).start()

    W = 128
    pieces = [(0, k) for k in range(gout_ref.shape[0] // W)] + [(1, k) for k in range(gin_ref.shape[0] // W)]
    half = nz // 2 * T

    def grad_piece(piece, r, add):
        which, k = piece
        c = slice(k * W, (k + 1) * W)
        if which == 0:
            ref, value = gout, mm(hid[0, r, c], tc[1, r, :], TN)
        else:
            ref, value = gin, mm(tc[0, r, c], hid[1, r, :], TN)
        ref[c, :] = ref[c, :] + value if add else value

    stops = sorted({e for e in (2, 4, 6, 7) if e < J} | {J})
    top = nz
    waiting = list(pieces)
    near = 0
    for j in range(1, J + 1):
        for i in range(2):
            forward(i, j)
        if j in stops:
            for n in range(near, j):
                for i in range(2):
                    for d in range(2):
                        hnear(d, i, n).wait_recv()
            near = j
            low = nz - 1 - 4 * j if j < J else 0
            products(low, top)
            top = low
        if J // 2 < j < J:
            for piece in waiting[:3]:
                grad_piece(piece, slice(half, 2 * half), False)
            waiting = waiting[3:]
    for piece in waiting:
        grad_piece(piece, slice(half, 2 * half), False)
    stores = []

    def put(src, dst):
        stores.append(pltpu.make_async_copy(src, dst, store_sem.at[len(stores)]))
        stores[-1].start()

    for piece in pieces:
        grad_piece(piece, slice(0, half), True)
        c = slice(piece[1] * W, (piece[1] + 1) * W)
        if piece[0] == 0:
            put(gout.at[c], gout_ref.at[c])
        else:
            put(gin.at[c], gin_ref.at[c])

    for p in range(nz):
        ocopy_self(p).wait()
    for i, ref in enumerate((out_ref, gtok_ref)):
        total = own[i].astype(F32)
        for p in range(nz):
            total = total + orecv[i, rows(p), :].astype(F32)
        ends[i] = total.astype(BF)
        put(ends.at[i], ref)

    @pl.loop(0, nz)
    def _(p):
        @pl.when(owner(p) != 0)
        def _():
            gather(p, row).wait_send()
            ocopy(p, row).wait_send()

    for i in range(2):
        for d in range(2):
            @pl.loop(0, S)
            def _(slot):
                @pl.when(slot >= d)
                def _():
                    zcopy(d, i, slot, side).wait_send()

            for j in range(J):
                hnear(d, i, j).wait_send()
                if j < last(d):
                    hfar(d, i, j).wait_send()
    for copy in stores:
        copy.wait()


def store(*refs):
    copies = [pltpu.make_async_copy(refs[i], refs[4 + i], refs[8].at[i]) for i in range(4)]
    for copy in copies:
        copy.start()
    for copy in copies:
        copy.wait()


def on_device(nz, dims, tokens, w_in, w_out, cotangent):
    T, DL = tokens.shape
    HL = w_in.shape[1]
    S = nz // 2
    hbm = pl.BlockSpec(memory_space=pltpu.HBM)
    dma = pltpu.SemaphoreType.DMA
    flops = 2 * 6 * nz * T * DL * HL
    outs = (
        jax.ShapeDtypeStruct((T, DL), BF),
        jax.ShapeDtypeStruct((T, DL), BF),
        jax.ShapeDtypeStruct((DL, HL), F32),
        jax.ShapeDtypeStruct((HL, DL), F32),
    )
    results = pl.pallas_call(
        functools.partial(kernel, nz, dims, T),
        out_shape=outs,
        in_specs=[hbm] * 4,
        out_specs=(hbm,) * 4,
        scratch_shapes=[
            pltpu.VMEM((2, T, DL), BF),
            pltpu.VMEM((2, nz * T, DL), BF),
            pltpu.VMEM((DL, HL), BF),
            pltpu.VMEM((HL, DL), BF),
            pltpu.VMEM((2, nz * T, HL), F32),
            pltpu.VMEM((2, 2, S * T, HL), BF),
            pltpu.VMEM((2, 2, S * T, HL), BF),
            pltpu.VMEM((2, nz * T, HL), BF),
            pltpu.VMEM((2, nz * T, DL), BF),
            pltpu.VMEM((2, nz * T, DL), BF),
            pltpu.VMEM((DL, HL), F32),
            pltpu.VMEM((HL, DL), F32),
            pltpu.VMEM((2, T, DL), BF),
            dma((4,)),
            dma((nz,)),
            dma((nz,)),
            dma((2, 2, S)),
            dma((2, 2, S)),
            dma((2, 2, S)),
            dma((2, 2, S)),
            dma((nz,)),
            dma((nz,)),
            dma((2 + (DL + HL) // 128,)),
        ],
        compiler_params=pltpu.CompilerParams(
            collective_id=0, has_side_effects=True, vmem_limit_bytes=58 * 2**20
        ),
        cost_estimate=pl.CostEstimate(flops=flops, bytes_accessed=4 * DL * HL * 3, transcendentals=0),
    )(tokens, cotangent, w_in, w_out)
    return pl.pallas_call(
        store,
        out_shape=outs,
        in_specs=[pl.BlockSpec(memory_space=pl.ANY)] * 4,
        out_specs=(hbm,) * 4,
        scratch_shapes=[dma((4,))],
        compiler_params=pltpu.CompilerParams(vmem_limit_bytes=58 * 2**20),
    )(*results)


def solution(mesh):
    nz = mesh.shape["col"]
    dims = {32: (4, 4, 2), 8: (2, 2, 2), 4: (1, 2, 2)}[mesh.shape["row"]]
    return jax.shard_map(
        functools.partial(on_device, nz, dims),
        mesh=mesh,
        in_specs=(P("row", "col"), P("col", "row"), P("row", "col"), P("row", "col")),
        out_specs=(P("row", "col"), P("row", "col"), P("col", "row"), P("row", "col")),
        check_vma=False,
    )
```

time: 148 us -> 188 us (1.27)
  Pallas kernels: 139 us -> 187 us
  local copies, waits for them, and re-layouts: 6.76 us -> 0 us
    pallas_call x1 -> x2, Pallas kernels: 139 us -> 187 us  [the longest x1 113 us: on_device(): pl.pallas_call(functools.partial(kernel, nz, dims, T), out_shape=outs, in...]
    unnamed x12 -> x0, local copies, waits for them, and re-layouts: 6.76 us -> none
where the time goes in v2:
time: 188 us; the launch traced here: 187 us
  Pallas kernels  187 us (99%)
    pallas_call x1, Pallas kernels, on_device(): pl.pallas_call(functools.partial(kernel, nz, dims, T), out_shape=outs, in...  113 us
    pallas_call x1, Pallas kernels, on_device(): pl.pallas_call(store, out_shape=outs, in_specs=[pl.BlockSpec(memory_space...  73.4 us

profile of v2, /device:TPU:1, one launch (start us, length us, event | category | flops | bytes accessed | tf_op | source)
XLA Modules:
  0.0 187.3 jit_solution(9020295271181382912)
XLA Ops:
  0.6 113.3 %shard_map.75 = (bf16[16,384]{1,0:T(8,128)(2,1)}, bf16[16,384]{1,0:T(8,128)(2,1)}, f32[384,768]{1,0:T(8,128)}, f32[768,384]{1,0:T(8,128)}) custom-call(bf16[16,384]{1,0:T(8,128)(2,1)} %tok_ref.1, bf16[16,384]{1,0:T(8,128)(2,1)} %cot_ref.1, bf16[384,768]{1,0:T(8,128)(2,1)} %win_ref.1, bf16[768,384]{1,0:T(8,128)(2,1)} %wout_ref.1), custom_call_target="tpu_custom_call" | custom-call | flops 1811939328 | bytes 3538944 | tf_op jit(solution)/shard_map/pallas_call | solution.py:351
  113.9 73.4 %shard_map.76 = (bf16[16,384]{1,0:T(8,128)(2,1)}, bf16[16,384]{1,0:T(8,128)(2,1)}, f32[384,768]{1,0:T(8,128)}, f32[768,384]{1,0:T(8,128)}) custom-call(bf16[16,384]{1,0:T(8,128)(2,1)} %get-tuple-element.8.refs_0_, bf16[16,384]{1,0:T(8,128)(2,1)} %get-tuple-element.9.refs_1_, f32[384,768]{1,0:T(8,128)} %get-tuple-element.10.refs_2_, ...), custom_call_target="tpu_custom_call" | custom-call | tf_op jit(solution)/shard_map/pallas_call | solution.py:386

commit v3 on v2

--- a/solution.py
+++ b/solution.py
@@ -47,29 +47,21 @@
 
 
 def kernel(
-    nz, dims, T,
+    nz, T,
     tok_ref, cot_ref, win_ref, wout_ref,
     out_ref, gtok_ref, gin_ref, gout_ref,
     own, tc, win, wout, part, zsend, zrecv, hid, osend, orecv, gin, gout, ends,
     load_sem, gsend_sem, grecv_sem, zsend_sem, zrecv_sem, hsend_sem, hrecv_sem, osend_sem, orecv_sem, store_sem,
 ):
     row, z = lax.axis_index("row"), lax.axis_index("col")
-    X, Y, C = dims
     S = nz // 2
     J = S // 2
 
-    def digits(i):
-        return lax.div(i, Y * C), lax.rem(lax.div(i, C), Y), lax.rem(i, C)
-
-    rx, ry, rc = digits(row)
-
     def plus(o):
-        ox, oy, oc = digits(o)
-        return (lax.rem(rx + ox, X) * Y + lax.rem(ry + oy, Y)) * C + lax.rem(rc + oc, C)
+        return lax.rem(row + o, nz)
 
     def minus(o):
-        ox, oy, oc = digits(o)
-        return (lax.rem(rx - ox + X, X) * Y + lax.rem(ry - oy + Y, Y)) * C + lax.rem(rc - oc + C, C)
+        return lax.rem(row - o + nz, nz)
 
     def owner(p):
         half = lax.div(p + 1, 2)
@@ -110,17 +102,20 @@
     def gather_self(p):
         return pltpu.make_async_copy(own, tc.at[:, rows(p)], grecv_sem.at[p])
 
-    @pl.loop(0, nz)
-    def _(p):
-        o = owner(p)
-
-        @pl.when(o != 0)
-        def _():
-            gather(p, minus(o)).start()
-
-        @pl.when(o == 0)
-        def _():
-            gather_self(p).start()
+    def spread(lo, hi):
+        @pl.loop(lo, hi)
+        def _(p):
+            o = owner(p)
+
+            @pl.when(o != 0)
+            def _():
+                gather(p, minus(o)).start()
+
+            @pl.when(o == 0)
+            def _():
+                gather_self(p).start()
+
+    spread(0, min(8, nz))
 
     for i, (src, dst) in ((2, (win_ref, win)), (3, (wout_ref, wout))):
         pltpu.make_async_copy(src, dst, load_sem.at[i]).wait()
@@ -145,7 +140,7 @@
         zcopy(d, i, slot, side).wait_recv()
         return decode(zrecv[d, i, rows(slot), :])
 
-    def zstep(j, first):
+    def zfar(j, first):
         for i in range(2):
             for d in range(2):
                 if first == 0 and d == 1:
@@ -157,22 +152,34 @@
                     value = value + arrived(d, i, j - 1)
                 zsend[d, i, rows(j), :] = encode(value)
                 zcopy(d, i, j, far).start()
+
+    def znear(j):
         for i in range(2):
             for d in range(2):
                 zsend[d, i, rows(J + j), :] = encode(part[i, rows(4 * j + 2 - d), :])
                 zcopy(d, i, J + j, side).start()
 
+    def zstep(j, first):
+        znear(j)
+        zfar(j, first)
+
     partials(0, 4)
-    zstep(0, 0)
-    done = 0
-    for lo, hi in ((4, 8), (8, 16), (16, nz)):
-        if hi <= nz and lo < hi:
-            partials(lo, hi)
-            if done + 1 < J:
-                done += 1
-                zstep(done, min(done, 2))
-    if done + 1 < J:
-        pl.loop(done + 1, J)(lambda j: zstep(j, 2))
+    zfar(0, 0)
+    znear(0)
+    if J > 1:
+        if nz > 8:
+            spread(8, 16)
+        partials(4, 8)
+        zstep(1, 1)
+    if J > 2:
+        if nz > 16:
+            spread(16, nz)
+        partials(8, 16)
+        zstep(2, 2)
+        zstep(3, 2)
+    if J > 4:
+        partials(16, nz)
+        pl.loop(4, J)(lambda j: zstep(j, 2))
 
     def hslot(d, k):
         return 2 * (S - k) - 1 + (d if k else 0)
@@ -259,28 +266,39 @@
             ref, value = gin, mm(tc[0, r, c], hid[1, r, :], TN)
         ref[c, :] = ref[c, :] + value if add else value
 
-    stops = sorted({e for e in (2, 4, 6, 7) if e < J} | {J})
     top = nz
     waiting = list(pieces)
     near = 0
+
+    def ready(n):
+        nonlocal near
+        for k in range(near, n):
+            for i in range(2):
+                for d in range(2):
+                    hnear(d, i, k).wait_recv()
+        near = n
+
+    def multiply(low):
+        nonlocal top
+        if low < top:
+            products(low, top)
+            top = low
+
     for j in range(1, J + 1):
         for i in range(2):
             forward(i, j)
-        if j in stops:
-            for n in range(near, j):
-                for i in range(2):
-                    for d in range(2):
-                        hnear(d, i, n).wait_recv()
-            near = j
-            low = nz - 1 - 4 * j if j < J else 0
-            products(low, top)
-            top = low
-        if J // 2 < j < J:
+        if j % 2 == 1 and j >= 3 or j == J:
+            ready(j - 1)
+            multiply(nz - 1 - 4 * (j - 1))
+        if top <= nz // 2 and j < J:
             for piece in waiting[:3]:
                 grad_piece(piece, slice(half, 2 * half), False)
             waiting = waiting[3:]
+    ready(J)
+    multiply(0)
     for piece in waiting:
         grad_piece(piece, slice(half, 2 * half), False)
+
     stores = []
 
     def put(src, dst):
@@ -328,14 +346,28 @@
 
 
 def store(*refs):
-    copies = [pltpu.make_async_copy(refs[i], refs[4 + i], refs[8].at[i]) for i in range(4)]
-    for copy in copies:
-        copy.start()
-    for copy in copies:
-        copy.wait()
-
-
-def on_device(nz, dims, tokens, w_in, w_out, cotangent):
+    sources, targets, held, sems = refs[:4], refs[4:8], refs[8:12], refs[12]
+    moves = []
+    for source, target, block in zip(sources, targets, held):
+        height = min(128, source.shape[0])
+        for top in range(0, source.shape[0], height):
+            c, n = pl.ds(top, height), len(moves)
+            moves.append(
+                (
+                    pltpu.make_async_copy(source.at[c], block.at[c], sems.at[0, n]),
+                    pltpu.make_async_copy(block.at[c], target.at[c], sems.at[1, n]),
+                )
+            )
+    for load, _ in moves:
+        load.start()
+    for load, save in moves:
+        load.wait()
+        save.start()
+    for _, save in moves:
+        save.wait()
+
+
+def on_device(nz, tokens, w_in, w_out, cotangent):
     T, DL = tokens.shape
     HL = w_in.shape[1]
     S = nz // 2
@@ -349,7 +381,7 @@
         jax.ShapeDtypeStruct((HL, DL), F32),
     )
     results = pl.pallas_call(
-        functools.partial(kernel, nz, dims, T),
+        functools.partial(kernel, nz, T),
         out_shape=outs,
         in_specs=[hbm] * 4,
         out_specs=(hbm,) * 4,
@@ -388,16 +420,15 @@
         out_shape=outs,
         in_specs=[pl.BlockSpec(memory_space=pl.ANY)] * 4,
         out_specs=(hbm,) * 4,
-        scratch_shapes=[dma((4,))],
+        scratch_shapes=[pltpu.VMEM(out.shape, out.dtype) for out in outs] + [dma((2, 2 + (DL + HL) // 128))],
         compiler_params=pltpu.CompilerParams(vmem_limit_bytes=58 * 2**20),
     )(*results)
 
 
 def solution(mesh):
     nz = mesh.shape["col"]
-    dims = {32: (4, 4, 2), 8: (2, 2, 2), 4: (1, 2, 2)}[mesh.shape["row"]]
     return jax.shard_map(
-        functools.partial(on_device, nz, dims),
+        functools.partial(on_device, nz),
         mesh=mesh,
         in_specs=(P("row", "col"), P("col", "row"), P("row", "col"), P("row", "col")),
         out_specs=(P("row", "col"), P("row", "col"), P("col", "row"), P("row", "col")),

time: 188 us -> 109 us (0.58)
  Pallas kernels: 187 us -> 108 us
    pallas_call x1, Pallas kernels: 73.4 us -> 2.61 us  [on_device(): pl.pallas_call(store, out_shape=outs, in_specs=[pl.BlockSpec(memory_space...]
    pallas_call x1, Pallas kernels: 113 us -> 106 us  [on_device(): pl.pallas_call(functools.partial(kernel, nz, T), out_shape=outs, in_specs...]
where the time goes in v3:
time: 109 us
  Pallas kernels  108 us (99%)
    pallas_call x1, Pallas kernels, on_device(): pl.pallas_call(functools.partial(kernel, nz, T), out_shape=outs, in_specs...  106 us
    pallas_call x1, Pallas kernels, on_device(): pl.pallas_call(store, out_shape=outs, in_specs=[pl.BlockSpec(memory_space...  2.61 us

profile of v3, /device:TPU:1, one launch (start us, length us, event | category | flops | bytes accessed | tf_op | source)
XLA Modules:
  0.0 109.1 jit_solution(17716313246841565368)
XLA Ops:
  0.6 105.8 %shard_map.75 = (bf16[16,384]{1,0:T(8,128)(2,1)}, bf16[16,384]{1,0:T(8,128)(2,1)}, f32[384,768]{1,0:T(8,128)}, f32[768,384]{1,0:T(8,128)}) custom-call(bf16[16,384]{1,0:T(8,128)(2,1)} %tok_ref.1, bf16[16,384]{1,0:T(8,128)(2,1)} %cot_ref.1, bf16[384,768]{1,0:T(8,128)(2,1)} %win_ref.1, bf16[768,384]{1,0:T(8,128)(2,1)} %wout_ref.1), custom_call_target="tpu_custom_call" | custom-call | flops 1811939328 | bytes 3538944 | tf_op jit(solution)/shard_map/pallas_call | solution.py:383
  106.5 2.6 %shard_map.76 = (bf16[16,384]{1,0:T(8,128)(2,1)}, bf16[16,384]{1,0:T(8,128)(2,1)}, f32[384,768]{1,0:T(8,128)}, f32[768,384]{1,0:T(8,128)}) custom-call(bf16[16,384]{1,0:T(8,128)(2,1)} %get-tuple-element.8.refs_0_, bf16[16,384]{1,0:T(8,128)(2,1)} %get-tuple-element.9.refs_1_, f32[384,768]{1,0:T(8,128)} %get-tuple-element.10.refs_2_, ...), custom_call_target="tpu_custom_call" | custom-call | tf_op jit(solution)/shard_map/pallas_call | solution.py:418

commit v4 on v3

--- a/solution.py
+++ b/solution.py
@@ -57,22 +57,27 @@
     S = nz // 2
     J = S // 2
 
+    def wrap(v):
+        return jnp.where(v >= nz, v - nz, v)
+
     def plus(o):
-        return lax.rem(row + o, nz)
+        return wrap(row + o)
 
     def minus(o):
-        return lax.rem(row - o + nz, nz)
+        return wrap(row - o + nz)
 
     def owner(p):
+        if isinstance(p, int):
+            k = S - p // 2 if p % 2 == 0 else nz + (p + 1) // 2 - S
+            return wrap(z + k % nz)
         half = lax.div(p + 1, 2)
-        off = jnp.where(lax.rem(p, 2) == 0, S - half, half - S)
-        return lax.rem(z + off + nz, nz)
+        return wrap(z + jnp.where(lax.rem(p, 2) == 0, S - half, wrap(half - S + nz)))
 
     def rows(p, n=1):
         return pl.ds(pl.multiple_of(p * T, T), n * T)
 
-    side = (lax.rem(z + 1, nz), lax.rem(z + nz - 1, nz))
-    far = (lax.rem(z + 2, nz), lax.rem(z + nz - 2, nz))
+    side = (wrap(z + 1), wrap(z + nz - 1))
+    far = (wrap(z + 2), wrap(z + nz - 2))
     ring = side + (far if nz > 4 else far[:1])
 
     for i, (src, dst) in enumerate(
@@ -102,9 +107,9 @@
     def gather_self(p):
         return pltpu.make_async_copy(own, tc.at[:, rows(p)], grecv_sem.at[p])
 
-    def spread(lo, hi):
-        @pl.loop(lo, hi)
-        def _(p):
+    def spread(lo, n):
+        for k in range(n):
+            p = lo + k
             o = owner(p)
 
             @pl.when(o != 0)
@@ -116,16 +121,13 @@
                 gather_self(p).start()
 
     spread(0, min(8, nz))
-
     for i, (src, dst) in ((2, (win_ref, win)), (3, (wout_ref, wout))):
         pltpu.make_async_copy(src, dst, load_sem.at[i]).wait()
 
-    def partials(lo, hi):
-        @pl.loop(lo, hi)
-        def _(p):
-            gather_self(p).wait()
-
-        r = slice(lo * T, hi * T)
+    def partials(j):
+        for k in range(4):
+            gather_self(4 * j + k).wait()
+        r = rows(4 * j, 4)
         part[0, r, :] = mm(tc[0, r, :], win[...], NN)
         part[1, r, :] = mm(tc[1, r, :], wout[...], NT)
 
@@ -160,26 +162,28 @@
                 zcopy(d, i, J + j, side).start()
 
     def zstep(j, first):
+        partials(j)
         znear(j)
         zfar(j, first)
 
-    partials(0, 4)
+    partials(0)
     zfar(0, 0)
     znear(0)
+    if J > 2:
+        spread(8, 4)
     if J > 1:
-        if nz > 8:
-            spread(8, 16)
-        partials(4, 8)
         zstep(1, 1)
     if J > 2:
-        if nz > 16:
-            spread(16, nz)
-        partials(8, 16)
-        zstep(2, 2)
-        zstep(3, 2)
-    if J > 4:
-        partials(16, nz)
-        pl.loop(4, J)(lambda j: zstep(j, 2))
+        if J > 3:
+            spread(12, 4)
+
+        @pl.loop(2, J)
+        def _(j):
+            @pl.when(j < J - 2)
+            def _():
+                spread(4 * j + 8, 4)
+
+            zstep(j, 2)
 
     def hslot(d, k):
         return 2 * (S - k) - 1 + (d if k else 0)
@@ -240,9 +244,7 @@
         osend[0, r, :] = mm(hid[0, r, :], wout[...], NN).astype(BF)
         osend[1, r, :] = mm(hid[1, r, :], win[...], NT).astype(BF)
 
-        @pl.loop(lo, hi)
-        def _(j):
-            p = lo + hi - 1 - j
+        for p in reversed(range(lo, hi)):
             o = owner(p)
 
             @pl.when(o != 0)
@@ -284,16 +286,40 @@
             products(low, top)
             top = low
 
+    def left(j):
+        if j == 1:
+            @pl.loop(0, nz)
+            def _(p):
+                @pl.when(owner(p) != 0)
+                def _():
+                    gather(p, row).wait_send()
+        if 2 <= j <= 3 or J < 3 and j == J:
+            for d in ((0, 1) if J < 3 else (j - 2,)):
+                for i in range(2):
+                    pl.loop(0, J)(lambda slot: zcopy(d, i, J + slot, side).wait_send())
+                    pl.loop(d, J)(lambda slot: zcopy(d, i, slot, far).wait_send())
+
+    def passed(j):
+        for i in range(2):
+            for d in range(2):
+                if j < J:
+                    hnear(d, i, j).wait_send()
+                if j < last(d):
+                    hfar(d, i, j).wait_send()
+
     for j in range(1, J + 1):
         for i in range(2):
             forward(i, j)
-        if j % 2 == 1 and j >= 3 or j == J:
+        if j > 1:
             ready(j - 1)
             multiply(nz - 1 - 4 * (j - 1))
         if top <= nz // 2 and j < J:
-            for piece in waiting[:3]:
+            for piece in waiting[:4]:
                 grad_piece(piece, slice(half, 2 * half), False)
-            waiting = waiting[3:]
+            waiting = waiting[4:]
+        left(j)
+        if j > 2:
+            passed(j - 3)
     ready(J)
     multiply(0)
     for piece in waiting:
@@ -313,7 +339,7 @@
         else:
             put(gin.at[c], gin_ref.at[c])
 
-    for p in range(nz):
+    for p in reversed(range(nz)):
         ocopy_self(p).wait()
     for i, ref in enumerate((out_ref, gtok_ref)):
         total = own[i].astype(F32)
@@ -322,25 +348,15 @@
         ends[i] = total.astype(BF)
         put(ends.at[i], ref)
 
+    for j in range(max(J - 2, 0), J):
+        passed(j)
+
     @pl.loop(0, nz)
     def _(p):
         @pl.when(owner(p) != 0)
         def _():
-            gather(p, row).wait_send()
             ocopy(p, row).wait_send()
 
-    for i in range(2):
-        for d in range(2):
-            @pl.loop(0, S)
-            def _(slot):
-                @pl.when(slot >= d)
-                def _():
-                    zcopy(d, i, slot, side).wait_send()
-
-            for j in range(J):
-                hnear(d, i, j).wait_send()
-                if j < last(d):
-                    hfar(d, i, j).wait_send()
     for copy in stores:
         copy.wait()
 

time: 109 us -> 108 us (level)
  no operation moved by 1% of the time
where the time goes in v4:
time: 108 us
  Pallas kernels  107 us (99%)
    pallas_call x1, Pallas kernels, on_device(): pl.pallas_call(functools.partial(kernel, nz, T), out_shape=outs, in_specs...  105 us
    pallas_call x1, Pallas kernels, on_device(): pl.pallas_call(store, out_shape=outs, in_specs=[pl.BlockSpec(memory_space...  2.61 us

profile of v4, /device:TPU:1, one launch (start us, length us, event | category | flops | bytes accessed | tf_op | source)
XLA Modules:
  0.0 108.1 jit_solution(5122761812511705893)
XLA Ops:
  0.6 104.8 %shard_map.75 = (bf16[16,384]{1,0:T(8,128)(2,1)}, bf16[16,384]{1,0:T(8,128)(2,1)}, f32[384,768]{1,0:T(8,128)}, f32[768,384]{1,0:T(8,128)}) custom-call(bf16[16,384]{1,0:T(8,128)(2,1)} %tok_ref.1, bf16[16,384]{1,0:T(8,128)(2,1)} %cot_ref.1, bf16[384,768]{1,0:T(8,128)(2,1)} %win_ref.1, bf16[768,384]{1,0:T(8,128)(2,1)} %wout_ref.1), custom_call_target="tpu_custom_call" | custom-call | flops 1811939328 | bytes 3538944 | tf_op jit(solution)/shard_map/pallas_call | solution.py:399
  105.5 2.6 %shard_map.76 = (bf16[16,384]{1,0:T(8,128)(2,1)}, bf16[16,384]{1,0:T(8,128)(2,1)}, f32[384,768]{1,0:T(8,128)}, f32[768,384]{1,0:T(8,128)}) custom-call(bf16[16,384]{1,0:T(8,128)(2,1)} %get-tuple-element.8.refs_0_, bf16[16,384]{1,0:T(8,128)(2,1)} %get-tuple-element.9.refs_1_, f32[384,768]{1,0:T(8,128)} %get-tuple-element.10.refs_2_, ...), custom_call_target="tpu_custom_call" | custom-call | tf_op jit(solution)/shard_map/pallas_call | solution.py:434

commit v5 on v4

--- a/solution.py
+++ b/solution.py
@@ -138,6 +138,18 @@
             device_id=(row, peer[d]), device_id_type=MESH,
         )
 
+    def znext(d, j):
+        return pltpu.make_async_remote_copy(
+            src_ref=zsend.at[d, :, rows(J + j)], dst_ref=zrecv.at[d, :, rows(J + j)],
+            send_sem=zsend_sem.at[d, 0, J + j], recv_sem=zrecv_sem.at[d, 0, J + j],
+            device_id=(row, side[d]), device_id_type=MESH,
+        )
+
+    def beside(d, i, j):
+        if i == 0:
+            znext(d, j).wait_recv()
+        return decode(zrecv[d, i, rows(J + j), :])
+
     def arrived(d, i, slot):
         zcopy(d, i, slot, side).wait_recv()
         return decode(zrecv[d, i, rows(slot), :])
@@ -149,17 +161,17 @@
                     continue
                 value = part[i, rows(4 * j - d), :]
                 if first > 0:
-                    value = value + arrived(d, i, J + j - 1)
+                    value = value + beside(d, i, j - 1)
                 if first > d:
                     value = value + arrived(d, i, j - 1)
                 zsend[d, i, rows(j), :] = encode(value)
                 zcopy(d, i, j, far).start()
 
     def znear(j):
-        for i in range(2):
-            for d in range(2):
+        for d in range(2):
+            for i in range(2):
                 zsend[d, i, rows(J + j), :] = encode(part[i, rows(4 * j + 2 - d), :])
-                zcopy(d, i, J + j, side).start()
+            znext(d, j).start()
 
     def zstep(j, first):
         partials(j)
@@ -195,10 +207,10 @@
             device_id=(row, far[d]), device_id_type=MESH,
         )
 
-    def hnear(d, i, j):
-        return pltpu.make_async_remote_copy(
-            src_ref=hid.at[i, rows(hslot(d, 2 * j))], dst_ref=hid.at[i, rows(hslot(d, 2 * j + 1))],
-            send_sem=hsend_sem.at[d, i, J + j], recv_sem=hrecv_sem.at[d, i, J + j],
+    def hnear(d, j):
+        return pltpu.make_async_remote_copy(
+            src_ref=hid.at[:, rows(hslot(d, 2 * j))], dst_ref=hid.at[:, rows(hslot(d, 2 * j + 1))],
+            send_sem=hsend_sem.at[d, 0, J + j], recv_sem=hrecv_sem.at[d, 0, J + j],
             device_id=(row, side[d]), device_id_type=MESH,
         )
 
@@ -211,15 +223,15 @@
                 hfar(d, i, j - 1).wait_recv()
             if j < last(d):
                 hfar(d, i, j).start()
-            if j < J:
-                hnear(d, i, j).start()
+            if j < J and i == 1:
+                hnear(d, j).start()
 
     own_rows = rows(nz - 1)
     slope = None
     for i in range(2):
         value = part[i, own_rows, :]
         for d in range(2):
-            value = value + arrived(d, i, 2 * J - 1)
+            value = value + beside(d, i, J - 1)
             if J - 1 >= d:
                 value = value + arrived(d, i, J - 1)
         if i == 0:
@@ -275,9 +287,8 @@
     def ready(n):
         nonlocal near
         for k in range(near, n):
-            for i in range(2):
-                for d in range(2):
-                    hnear(d, i, k).wait_recv()
+            for d in range(2):
+                hnear(d, k).wait_recv()
         near = n
 
     def multiply(low):
@@ -295,15 +306,15 @@
                     gather(p, row).wait_send()
         if 2 <= j <= 3 or J < 3 and j == J:
             for d in ((0, 1) if J < 3 else (j - 2,)):
+                pl.loop(0, J)(lambda j: znext(d, j).wait_send())
                 for i in range(2):
-                    pl.loop(0, J)(lambda slot: zcopy(d, i, J + slot, side).wait_send())
                     pl.loop(d, J)(lambda slot: zcopy(d, i, slot, far).wait_send())
 
     def passed(j):
         for i in range(2):
             for d in range(2):
-                if j < J:
-                    hnear(d, i, j).wait_send()
+                if j < J and i == 0:
+                    hnear(d, j).wait_send()
                 if j < last(d):
                     hfar(d, i, j).wait_send()
 

time: 108 us -> 108 us (level)
  no operation moved by 1% of the time
where the time goes in v5:
time: 108 us
  Pallas kernels  107 us (99%)
    pallas_call x1, Pallas kernels, on_device(): pl.pallas_call(functools.partial(kernel, nz, T), out_shape=outs, in_specs...  105 us
    pallas_call x1, Pallas kernels, on_device(): pl.pallas_call(store, out_shape=outs, in_specs=[pl.BlockSpec(memory_space...  2.61 us

profile of v5, /device:TPU:1, one launch (start us, length us, event | category | flops | bytes accessed | tf_op | source)
XLA Modules:
  0.0 107.8 jit_solution(12860332603418615311)
XLA Ops:
  0.6 104.6 %shard_map.75 = (bf16[16,384]{1,0:T(8,128)(2,1)}, bf16[16,384]{1,0:T(8,128)(2,1)}, f32[384,768]{1,0:T(8,128)}, f32[768,384]{1,0:T(8,128)}) custom-call(bf16[16,384]{1,0:T(8,128)(2,1)} %tok_ref.1, bf16[16,384]{1,0:T(8,128)(2,1)} %cot_ref.1, bf16[384,768]{1,0:T(8,128)(2,1)} %win_ref.1, bf16[768,384]{1,0:T(8,128)(2,1)} %wout_ref.1), custom_call_target="tpu_custom_call" | custom-call | flops 1811939328 | bytes 3538944 | tf_op jit(solution)/shard_map/pallas_call | solution.py:410
  105.2 2.6 %shard_map.76 = (bf16[16,384]{1,0:T(8,128)(2,1)}, bf16[16,384]{1,0:T(8,128)(2,1)}, f32[384,768]{1,0:T(8,128)}, f32[768,384]{1,0:T(8,128)}) custom-call(bf16[16,384]{1,0:T(8,128)(2,1)} %get-tuple-element.8.refs_0_, bf16[16,384]{1,0:T(8,128)(2,1)} %get-tuple-element.9.refs_1_, f32[384,768]{1,0:T(8,128)} %get-tuple-element.10.refs_2_, ...), custom_call_target="tpu_custom_call" | custom-call | tf_op jit(solution)/shard_map/pallas_call | solution.py:445
